TPU v7x, 32 devices: a whole 2x2x4 slice. The times are simulated.
32 devices in a mesh: geom: 2 (over y), gx: 4 (over z), gy: 2 (over x), gz: 2 (over core).
Axes of the slice: x: 2, y: 2, z: 4, core: 2. Of those that a mesh axis runs over, the one named last changes fastest.
Arguments:
- features: bfloat16 [20480, 128], P(('geom', 'gx', 'gy', 'gz')), parts along dimension 0, may hold values from -6 to 6
- displacement: float32 [3, 983040], P(None, ('geom', 'gx', 'gy', 'gz')), parts along dimension 1, as said below
- neighbour: int32 [983040], P(('geom', 'gx', 'gy', 'gz')), parts along dimension 0, may hold values from 0 to 2687, as said below
- neighbour_count: int32 [20480], P(('geom', 'gx', 'gy', 'gz')), parts along dimension 0, may hold values from 12 to 48, as said below
- species: int32 [20480], P(('geom', 'gx', 'gy', 'gz')), parts along dimension 0, may hold values from 0 to 99
- exports_x: int32 [32, 2, 640], P(('geom', 'gx', 'gy', 'gz')), parts along dimension 0, may hold values from 0 to 639, as said below
- exports_y: int32 [32, 2, 256], P(('geom', 'gx', 'gy', 'gz')), parts along dimension 0, may hold values from 0 to 639, as said below
- exports_z: int32 [32, 2, 128], P(('geom', 'gx', 'gy', 'gz')), parts along dimension 0, may hold values from 0 to 639, as said below
- face_counts: int32 [32, 6], P(('geom', 'gx', 'gy', 'gz')), parts along dimension 0, may hold values from 1 to 640, as said below
- w_in: bfloat16 [128, 128], replicated, may hold values from -0.5 to 0.5
- w_f1: bfloat16 [50, 128], replicated, may hold values from -1.75 to 1.75
- b_f1: float32 [128], replicated, may hold values from -3 to 3
- w_f2: bfloat16 [128, 128], replicated, may hold values from -0.125 to 0.125
- b_f2: float32 [128], replicated, may hold values from -3 to 3
- w_o1: bfloat16 [128, 128], replicated, may hold values from -0.5 to 0.5
- b_o1: float32 [128], replicated, may hold values from -3 to 3
- w_o2: bfloat16 [128, 128], replicated, may hold values from -0.5 to 0.5
- b_o2: float32 [128], replicated, may hold values from -3 to 3
- w_e1: bfloat16 [128, 64], replicated, may hold values from -0.5 to 0.5
- b_e1: float32 [64], replicated, may hold values from -3 to 3
- w_e2: float32 [64], replicated, may hold values from -1.5 to 1.5
- species_scale: float32 [100], replicated, may hold values from 0.5 to 4
- species_shift: float32 [100], replicated, may hold values from -1 to 1
Outputs:
- energy: float32 [20480], P(('geom', 'gx', 'gy', 'gz')), parts along dimension 0
- forces: float32 [3, 20480], P(None, ('geom', 'gx', 'gy', 'gz')), parts along dimension 1
There are 2 independent parts, one for each index of `geom`. A program takes and returns all parts, laid end to end along the dimension named above; an argument that names none is the same for every part. Nothing has to cross between parts.
Inputs may be any that keep to these rules, and one draw needn't show every extreme that they name: `face_counts`: entry column f is the used length of that face's list: at most 640 for columns 0 and 1, 256 for 2 and 3, 128 for 4 and 5; in every column some domain uses its whole list. `exports_x`: each list row names distinct own atoms. `exports_y`: each list row names distinct own atoms. `exports_z`: each list row names distinct own atoms. `neighbour`: live slots name an own row or a ghost row below the used length of its block; slots beyond the live count hold arbitrary rows. `neighbour_count`: every domain has an atom with all 48 slots live. `displacement`: lengths lie between 0.9 and 4.9.
All inputs are finite; a program needn't handle non-finite values.
Results may differ from a plain program's by a relative error of at most 0.012.
Values may be sent and summed in bfloat16 or wider, within the bound.
A program may use at most 128 MiB of HBM per device.

v0:
```python
import math

import jax
import jax.numpy as jnp
from jax import lax
from jax.sharding import PartitionSpec as P

GAMMA = 10.0
CUTOFF = 5.0
LOG_TWO = math.log(2.0)
UNIT_ROWS = 64


def from_behind(x, axis, by):
    devices = lax.axis_size(axis)
    return lax.ppermute(x, axis, [(i, (i + by) % devices) for i in range(devices)])


def shifted_softplus(value):
    return jax.nn.softplus(value) - LOG_TWO


def spread_terms(pair_force, index_rows, table_rows):
    groups = (table_rows + UNIT_ROWS - 1) // UNIT_ROWS
    pair_total = index_rows.shape[0]
    negated = -pair_force
    high_part = negated.astype(jnp.bfloat16)
    remain = negated - high_part.astype(jnp.float32)
    middle_part = remain.astype(jnp.bfloat16)
    low_part = (remain - middle_part.astype(jnp.float32)).astype(jnp.bfloat16)
    parts = jnp.concatenate([high_part, middle_part, low_part], axis=0)
    lower_onehot = (
        (index_rows % UNIT_ROWS)[:, None] == jnp.arange(UNIT_ROWS, dtype=jnp.int32)[None, :]
    ).astype(jnp.bfloat16)
    placed = (lower_onehot[:, :, None] * parts.T[:, None, :]).reshape(pair_total, UNIT_ROWS * 9)
    upper_onehot = (
        (index_rows // UNIT_ROWS)[:, None] == jnp.arange(groups, dtype=jnp.int32)[None, :]
    ).astype(jnp.bfloat16)
    summed = lax.dot_general(
        upper_onehot, placed, (((0,), (0,)), ((), ())), preferred_element_type=jnp.float32
    )
    summed = jnp.sum(summed.reshape(groups * UNIT_ROWS, 3, 3), axis=1)
    return summed.T


def block_terms(
    table, feat_rows, disp_rows, index_rows, count_rows, scale_rows, shift_rows, weights
):
    w_f1, b_f1, w_f2, b_f2, w_o1, b_o1, w_o2, b_o2, w_e1, b_e1, w_e2 = weights
    row_count = feat_rows.shape[0]
    slot_count = index_rows.shape[0] // row_count
    width = feat_rows.shape[1]
    radial = w_f1.shape[0]
    distance = jnp.sqrt(jnp.sum(disp_rows * disp_rows, axis=0))
    centres = jnp.arange(radial, dtype=jnp.float32) * (CUTOFF / (radial - 1))
    offset = distance[None, :] - centres[:, None]
    basis_vals = jnp.exp(-GAMMA * offset * offset)
    basis_slope = -2.0 * GAMMA * offset * basis_vals
    phase_arg = jnp.pi * distance / CUTOFF
    envelope = 0.5 * (jnp.cos(phase_arg) + 1.0)
    envelope_slope = -0.5 * jnp.pi / CUTOFF * jnp.sin(phase_arg)
    slot_index = lax.broadcasted_iota(jnp.int32, (row_count, slot_count), 1)
    live_mask = (slot_index < count_rows[:, None]).astype(jnp.float32).reshape(-1)
    pre_act = (
        lax.dot_general(
            basis_vals.astype(jnp.bfloat16),
            w_f1,
            (((0,), (0,)), ((), ())),
            preferred_element_type=jnp.float32,
        )
        + b_f1
    )
    hidden = shifted_softplus(pre_act).astype(jnp.bfloat16)
    filter_out = jnp.dot(hidden, w_f2, preferred_element_type=jnp.float32) + b_f2
    pair_weight = filter_out * (envelope * live_mask)[:, None]
    neighbour_rows = table[index_rows].astype(jnp.float32)
    message = jnp.sum((neighbour_rows * pair_weight).reshape(row_count, slot_count, width), axis=1)
    out_pre = jnp.dot(message.astype(jnp.bfloat16), w_o1, preferred_element_type=jnp.float32) + b_o1
    out_mid = shifted_softplus(out_pre).astype(jnp.bfloat16)
    updated = (
        feat_rows.astype(jnp.float32)
        + jnp.dot(out_mid, w_o2, preferred_element_type=jnp.float32)
        + b_o2
    )
    energy_pre = (
        jnp.dot(updated.astype(jnp.bfloat16), w_e1, preferred_element_type=jnp.float32) + b_e1
    )
    energy = scale_rows * jnp.sum(shifted_softplus(energy_pre) * w_e2[None, :], axis=1) + shift_rows
    grad_head = (scale_rows[:, None] * w_e2[None, :] * jax.nn.sigmoid(energy_pre)).astype(
        jnp.bfloat16
    )
    grad_update = jnp.dot(grad_head, w_e1.T, preferred_element_type=jnp.float32).astype(
        jnp.bfloat16
    )
    grad_mid = (
        jnp.dot(grad_update, w_o2.T, preferred_element_type=jnp.float32) * jax.nn.sigmoid(out_pre)
    ).astype(jnp.bfloat16)
    grad_message = jnp.dot(grad_mid, w_o1.T, preferred_element_type=jnp.float32)
    pair_grad = (
        grad_message[:, None, :] * neighbour_rows.reshape(row_count, slot_count, width)
    ).reshape(-1, width) * live_mask[:, None]
    grad_filter = (pair_grad * envelope[:, None]).astype(jnp.bfloat16)
    grad_pre = (
        jnp.dot(grad_filter, w_f2.T, preferred_element_type=jnp.float32) * jax.nn.sigmoid(pre_act)
    ).astype(jnp.bfloat16)
    grad_basis = lax.dot_general(
        w_f1, grad_pre, (((1,), (1,)), ((), ())), preferred_element_type=jnp.float32
    )
    grad_dist = (
        jnp.sum(grad_basis * basis_slope, axis=0)
        + jnp.sum(pair_grad * filter_out, axis=1) * envelope_slope
    )
    pair_force = disp_rows * (grad_dist / distance)[None, :]
    own_force = jnp.sum(pair_force.reshape(3, row_count, slot_count), axis=2)
    block_spread = spread_terms(pair_force, index_rows, table.shape[0])
    return (energy, own_force, block_spread)


def export_rows(x_local, index_row, used):
    kept_mask = jnp.arange(index_row.shape[0], dtype=jnp.int32) < used
    atom_ids = jnp.arange(x_local.shape[0], dtype=jnp.int32)
    picker = ((index_row[:, None] == atom_ids[None, :]) & kept_mask[:, None]).astype(jnp.bfloat16)
    return jnp.dot(picker, x_local, preferred_element_type=jnp.float32).astype(jnp.bfloat16)


def add_returned(forces, returned, index_row, used):
    kept_mask = jnp.arange(index_row.shape[0], dtype=jnp.int32) < used
    values = jnp.where(kept_mask[None, :], returned, jnp.zeros_like(returned))
    atom_ids = jnp.arange(forces.shape[1], dtype=jnp.int32)
    placer = (index_row[:, None] == atom_ids[None, :]).astype(jnp.float32)
    return forces + jnp.dot(values, placer, precision=lax.Precision.HIGHEST)


def body(
    features,
    displacement,
    neighbour,
    neighbour_count,
    species,
    exports_x,
    exports_y,
    exports_z,
    face_counts,
    w_in,
    w_f1,
    b_f1,
    w_f2,
    b_f2,
    w_o1,
    b_o1,
    w_o2,
    b_o2,
    w_e1,
    b_e1,
    w_e2,
    species_scale,
    species_shift,
):
    atom_rows = features.shape[0]
    width = features.shape[1]
    slot_count = neighbour.shape[0] // atom_rows
    used_counts = face_counts[0]
    x_local = jnp.dot(features, w_in, preferred_element_type=jnp.float32).astype(jnp.bfloat16)
    lower_send_x = export_rows(x_local, exports_x[0, 0], used_counts[0])
    upper_send_x = export_rows(x_local, exports_x[0, 1], used_counts[1])
    lower_send_y = export_rows(x_local, exports_y[0, 0], used_counts[2])
    upper_send_y = export_rows(x_local, exports_y[0, 1], used_counts[3])
    lower_send_z = export_rows(x_local, exports_z[0, 0], used_counts[4])
    upper_send_z = export_rows(x_local, exports_z[0, 1], used_counts[5])
    from_lower_x = from_behind(upper_send_x, "gx", 1)
    from_upper_x = from_behind(lower_send_x, "gx", -1)
    from_lower_y = from_behind(upper_send_y, "gy", 1)
    from_upper_y = from_behind(lower_send_y, "gy", -1)
    from_lower_z = from_behind(upper_send_z, "gz", 1)
    from_upper_z = from_behind(lower_send_z, "gz", -1)
    table = jnp.concatenate(
        [
            x_local,
            from_lower_x,
            from_upper_x,
            from_lower_y,
            from_upper_y,
            from_lower_z,
            from_upper_z,
        ],
        axis=0,
    )
    kinds = species_scale.shape[0]
    species_onehot = (species[:, None] == jnp.arange(kinds, dtype=jnp.int32)[None, :]).astype(
        jnp.float32
    )
    scale_all = jnp.dot(species_onehot, species_scale, precision=lax.Precision.HIGHEST)
    shift_all = jnp.dot(species_onehot, species_shift, precision=lax.Precision.HIGHEST)
    block_rows = math.gcd(atom_rows, UNIT_ROWS)
    block_total = atom_rows // block_rows
    weights = (w_f1, b_f1, w_f2, b_f2, w_o1, b_o1, w_o2, b_o2, w_e1, b_e1, w_e2)

    def one_block(pieces):
        feat_rows, disp_rows, index_rows, count_rows, scale_rows, shift_rows = pieces
        return block_terms(
            table, feat_rows, disp_rows, index_rows, count_rows, scale_rows, shift_rows, weights
        )

    energy, own_force, block_spread = lax.map(
        one_block,
        (
            features.reshape(block_total, block_rows, width),
            displacement.reshape(3, block_total, block_rows * slot_count).transpose(1, 0, 2),
            neighbour.reshape(block_total, block_rows * slot_count),
            neighbour_count.reshape(block_total, block_rows),
            scale_all.reshape(block_total, block_rows),
            shift_all.reshape(block_total, block_rows),
        ),
    )
    energy = energy.reshape(-1)
    own_force = own_force.transpose(1, 0, 2).reshape(3, -1)
    spread = jnp.sum(block_spread, axis=0)
    forces = own_force + spread[:, :atom_rows]
    ghost_force = spread[:, atom_rows:]
    x_len = exports_x.shape[2]
    y_len = exports_y.shape[2]
    z_len = exports_z.shape[2]
    start_y = 2 * x_len
    start_z = 2 * x_len + 2 * y_len
    ghost_lower_x = ghost_force[:, 0:x_len]
    ghost_upper_x = ghost_force[:, x_len : 2 * x_len]
    ghost_lower_y = ghost_force[:, start_y : start_y + y_len]
    ghost_upper_y = ghost_force[:, start_y + y_len : start_y + 2 * y_len]
    ghost_lower_z = ghost_force[:, start_z : start_z + z_len]
    ghost_upper_z = ghost_force[:, start_z + z_len : start_z + 2 * z_len]
    mine_upper_x = from_behind(ghost_lower_x, "gx", -1)
    mine_lower_x = from_behind(ghost_upper_x, "gx", 1)
    mine_upper_y = from_behind(ghost_lower_y, "gy", -1)
    mine_lower_y = from_behind(ghost_upper_y, "gy", 1)
    mine_upper_z = from_behind(ghost_lower_z, "gz", -1)
    mine_lower_z = from_behind(ghost_upper_z, "gz", 1)
    forces = add_returned(forces, mine_upper_x, exports_x[0, 1], used_counts[1])
    forces = add_returned(forces, mine_lower_x, exports_x[0, 0], used_counts[0])
    forces = add_returned(forces, mine_upper_y, exports_y[0, 1], used_counts[3])
    forces = add_returned(forces, mine_lower_y, exports_y[0, 0], used_counts[2])
    forces = add_returned(forces, mine_upper_z, exports_z[0, 1], used_counts[5])
    forces = add_returned(forces, mine_lower_z, exports_z[0, 0], used_counts[4])
    return (energy, forces)


def solution(mesh):
    return jax.shard_map(
        body,
        mesh=mesh,
        in_specs=(
            P(("geom", "gx", "gy", "gz"), None),
            P(None, ("geom", "gx", "gy", "gz")),
            P(("geom", "gx", "gy", "gz")),
            P(("geom", "gx", "gy", "gz")),
            P(("geom", "gx", "gy", "gz")),
            P(("geom", "gx", "gy", "gz"), None, None),
            P(("geom", "gx", "gy", "gz"), None, None),
            P(("geom", "gx", "gy", "gz"), None, None),
            P(("geom", "gx", "gy", "gz"), None),
            P(),
            P(),
            P(),
            P(),
            P(),
            P(),
            P(),
            P(),
            P(),
            P(),
            P(),
            P(),
            P(),
            P(),
        ),
        out_specs=(P(("geom", "gx", "gy", "gz")), P(None, ("geom", "gx", "gy", "gz"))),
        check_vma=False,
    )
```

profile of v0, /device:TPU:0, one launch (start us, length us, event | category | flops | bytes accessed | tf_op | source)
XLA Modules:
  0.0 766.2 jit_solution(1715216590804499384)
XLA Ops:
  27.1 710.6 %while.17 = (s32[]{:T(128)}, f32[10,64]{1,0:T(8,128)}, f32[10,3,64]{2,1,0:T(4,128)}, f32[10,3,2688]{1,2,0:T(8,128)}, f32[10,64]{1,0:T(8,128)}, /*index=5*/bf16[1...) while((s32[]{:T(128)}, f32[10,64]{1,0:T(8,128)}, ...), condition=%wide.region_8.9_spmd, body=%wide.region_0.8_spmd.sunk | while | flops 454050496 | bytes 34617212 | solution.py:204
  33.8 9.2 %gather_fusion = bf16[3072,128]{1,0:T(8,128)(2,1)S(1)} fusion(bf16[2688,128]{1,0:T(8,128)(2,1)S(1)} %get-tuple-element.657, s32[3072]{0:T(1024)S(1)} %broadcast_clamp_fusion.2), kind=kCustom, calls=%fused_computation.clone.1 | custom fusion | bytes 1585152 | tf_op jit(solution)/shard_map/while/body/eval_jaxpr/gather | solution.py:76
  58.0 3.8 fusion.230
  68.3 7.5 mul.530
  75.8 3.5 fusion.234
  79.4 4.8 reshape.393
  84.2 12.9 %reduce_sum.129 = f32[2688,3]{1,0:T(8,128)S(1)} reduce(f32[2688,3,3]{2,1,0:T(4,128)} %reshape.393, f32[]{:T(128)} %constant.163.clone.1..sunk), dimensions={1}, to_apply=%region_7.7 | reduce | flops 16128 | bytes 129028 | tf_op jit(solution)/shard_map/while/body/eval_jaxpr/reduce_sum | solution.py:42
  104.9 9.2 %gather_fusion = bf16[3072,128]{1,0:T(8,128)(2,1)S(1)} fusion(bf16[2688,128]{1,0:T(8,128)(2,1)S(1)} %get-tuple-element.657, s32[3072]{0:T(1024)S(1)} %broadcast_clamp_fusion.2), kind=kCustom, calls=%fused_computation.clone.1 | custom fusion | bytes 1585152 | tf_op jit(solution)/shard_map/while/body/eval_jaxpr/gather | solution.py:76
  129.1 3.8 fusion.230
  139.4 7.5 mul.530
  146.9 3.5 fusion.234
  150.4 4.8 reshape.393
  155.3 12.9 %reduce_sum.129 = f32[2688,3]{1,0:T(8,128)S(1)} reduce(f32[2688,3,3]{2,1,0:T(4,128)} %reshape.393, f32[]{:T(128)} %constant.163.clone.1..sunk), dimensions={1}, to_apply=%region_7.7 | reduce | flops 16128 | bytes 129028 | tf_op jit(solution)/shard_map/while/body/eval_jaxpr/reduce_sum | solution.py:42
  175.9 9.2 %gather_fusion = bf16[3072,128]{1,0:T(8,128)(2,1)S(1)} fusion(bf16[2688,128]{1,0:T(8,128)(2,1)S(1)} %get-tuple-element.657, s32[3072]{0:T(1024)S(1)} %broadcast_clamp_fusion.2), kind=kCustom, calls=%fused_computation.clone.1 | custom fusion | bytes 1585152 | tf_op jit(solution)/shard_map/while/body/eval_jaxpr/gather | solution.py:76
  200.1 3.8 fusion.230
  210.4 7.5 mul.530
  217.9 3.5 fusion.234
  221.4 4.8 reshape.393
  226.3 12.9 %reduce_sum.129 = f32[2688,3]{1,0:T(8,128)S(1)} reduce(f32[2688,3,3]{2,1,0:T(4,128)} %reshape.393, f32[]{:T(128)} %constant.163.clone.1..sunk), dimensions={1}, to_apply=%region_7.7 | reduce | flops 16128 | bytes 129028 | tf_op jit(solution)/shard_map/while/body/eval_jaxpr/reduce_sum | solution.py:42
  246.9 9.2 %gather_fusion = bf16[3072,128]{1,0:T(8,128)(2,1)S(1)} fusion(bf16[2688,128]{1,0:T(8,128)(2,1)S(1)} %get-tuple-element.657, s32[3072]{0:T(1024)S(1)} %broadcast_clamp_fusion.2), kind=kCustom, calls=%fused_computation.clone.1 | custom fusion | bytes 1585152 | tf_op jit(solution)/shard_map/while/body/eval_jaxpr/gather | solution.py:76
  271.1 3.8 fusion.230
  281.4 7.5 mul.530
  288.9 3.5 fusion.234
  292.5 4.8 reshape.393
  297.3 12.9 %reduce_sum.129 = f32[2688,3]{1,0:T(8,128)S(1)} reduce(f32[2688,3,3]{2,1,0:T(4,128)} %reshape.393, f32[]{:T(128)} %constant.163.clone.1..sunk), dimensions={1}, to_apply=%region_7.7 | reduce | flops 16128 | bytes 129028 | tf_op jit(solution)/shard_map/while/body/eval_jaxpr/reduce_sum | solution.py:42
  318.0 9.2 %gather_fusion = bf16[3072,128]{1,0:T(8,128)(2,1)S(1)} fusion(bf16[2688,128]{1,0:T(8,128)(2,1)S(1)} %get-tuple-element.657, s32[3072]{0:T(1024)S(1)} %broadcast_clamp_fusion.2), kind=kCustom, calls=%fused_computation.clone.1 | custom fusion | bytes 1585152 | tf_op jit(solution)/shard_map/while/body/eval_jaxpr/gather | solution.py:76
  342.2 3.8 fusion.230
  352.5 7.5 mul.530
  360.0 3.5 fusion.234
  363.5 4.8 reshape.393
  368.4 12.9 %reduce_sum.129 = f32[2688,3]{1,0:T(8,128)S(1)} reduce(f32[2688,3,3]{2,1,0:T(4,128)} %reshape.393, f32[]{:T(128)} %constant.163.clone.1..sunk), dimensions={1}, to_apply=%region_7.7 | reduce | flops 16128 | bytes 129028 | tf_op jit(solution)/shard_map/while/body/eval_jaxpr/reduce_sum | solution.py:42
  389.0 9.2 %gather_fusion = bf16[3072,128]{1,0:T(8,128)(2,1)S(1)} fusion(bf16[2688,128]{1,0:T(8,128)(2,1)S(1)} %get-tuple-element.657, s32[3072]{0:T(1024)S(1)} %broadcast_clamp_fusion.2), kind=kCustom, calls=%fused_computation.clone.1 | custom fusion | bytes 1585152 | tf_op jit(solution)/shard_map/while/body/eval_jaxpr/gather | solution.py:76
  413.2 3.8 fusion.230
  423.5 7.5 mul.530
  431.0 3.5 fusion.234
  434.5 4.8 reshape.393
  439.4 12.9 %reduce_sum.129 = f32[2688,3]{1,0:T(8,128)S(1)} reduce(f32[2688,3,3]{2,1,0:T(4,128)} %reshape.393, f32[]{:T(128)} %constant.163.clone.1..sunk), dimensions={1}, to_apply=%region_7.7 | reduce | flops 16128 | bytes 129028 | tf_op jit(solution)/shard_map/while/body/eval_jaxpr/reduce_sum | solution.py:42
  460.1 9.2 %gather_fusion = bf16[3072,128]{1,0:T(8,128)(2,1)S(1)} fusion(bf16[2688,128]{1,0:T(8,128)(2,1)S(1)} %get-tuple-element.657, s32[3072]{0:T(1024)S(1)} %broadcast_clamp_fusion.2), kind=kCustom, calls=%fused_computation.clone.1 | custom fusion | bytes 1585152 | tf_op jit(solution)/shard_map/while/body/eval_jaxpr/gather | solution.py:76
  484.3 3.8 fusion.230
  494.6 7.5 mul.530
  502.1 3.5 fusion.234
  505.7 4.8 reshape.393
  510.5 12.9 %reduce_sum.129 = f32[2688,3]{1,0:T(8,128)S(1)} reduce(f32[2688,3,3]{2,1,0:T(4,128)} %reshape.393, f32[]{:T(128)} %constant.163.clone.1..sunk), dimensions={1}, to_apply=%region_7.7 | reduce | flops 16128 | bytes 129028 | tf_op jit(solution)/shard_map/while/body/eval_jaxpr/reduce_sum | solution.py:42
  531.2 9.2 %gather_fusion = bf16[3072,128]{1,0:T(8,128)(2,1)S(1)} fusion(bf16[2688,128]{1,0:T(8,128)(2,1)S(1)} %get-tuple-element.657, s32[3072]{0:T(1024)S(1)} %broadcast_clamp_fusion.2), kind=kCustom, calls=%fused_computation.clone.1 | custom fusion | bytes 1585152 | tf_op jit(solution)/shard_map/while/body/eval_jaxpr/gather | solution.py:76
  555.4 3.8 fusion.230
  565.7 7.5 mul.530
  573.2 3.5 fusion.234
  576.7 4.8 reshape.393
  581.6 12.9 %reduce_sum.129 = f32[2688,3]{1,0:T(8,128)S(1)} reduce(f32[2688,3,3]{2,1,0:T(4,128)} %reshape.393, f32[]{:T(128)} %constant.163.clone.1..sunk), dimensions={1}, to_apply=%region_7.7 | reduce | flops 16128 | bytes 129028 | tf_op jit(solution)/shard_map/while/body/eval_jaxpr/reduce_sum | solution.py:42
  602.2 9.2 %gather_fusion = bf16[3072,128]{1,0:T(8,128)(2,1)S(1)} fusion(bf16[2688,128]{1,0:T(8,128)(2,1)S(1)} %get-tuple-element.657, s32[3072]{0:T(1024)S(1)} %broadcast_clamp_fusion.2), kind=kCustom, calls=%fused_computation.clone.1 | custom fusion | bytes 1585152 | tf_op jit(solution)/shard_map/while/body/eval_jaxpr/gather | solution.py:76
  626.4 3.8 fusion.230
  636.6 7.5 mul.530
  644.2 3.5 fusion.234
  647.7 4.8 reshape.393
  652.6 12.9 %reduce_sum.129 = f32[2688,3]{1,0:T(8,128)S(1)} reduce(f32[2688,3,3]{2,1,0:T(4,128)} %reshape.393, f32[]{:T(128)} %constant.163.clone.1..sunk), dimensions={1}, to_apply=%region_7.7 | reduce | flops 16128 | bytes 129028 | tf_op jit(solution)/shard_map/while/body/eval_jaxpr/reduce_sum | solution.py:42
  673.2 9.2 %gather_fusion = bf16[3072,128]{1,0:T(8,128)(2,1)S(1)} fusion(bf16[2688,128]{1,0:T(8,128)(2,1)S(1)} %get-tuple-element.657, s32[3072]{0:T(1024)S(1)} %broadcast_clamp_fusion.2), kind=kCustom, calls=%fused_computation.clone.1 | custom fusion | bytes 1585152 | tf_op jit(solution)/shard_map/while/body/eval_jaxpr/gather | solution.py:76
  697.4 3.8 fusion.230
  707.7 7.5 mul.530
  718.8 4.8 reshape.393
  723.6 12.9 %reduce_sum.129 = f32[2688,3]{1,0:T(8,128)S(1)} reduce(f32[2688,3,3]{2,1,0:T(4,128)} %reshape.393, f32[]{:T(128)} %constant.163.clone.1..sunk), dimensions={1}, to_apply=%region_7.7 | reduce | flops 16128 | bytes 129028 | tf_op jit(solution)/shard_map/while/body/eval_jaxpr/reduce_sum | solution.py:42
  737.7 6.0 reduce_sum.106
  747.5 3.8 collective-permute-start.6
  754.4 5.5 collective-permute-done.7
  760.7 4.1 collective-permute-done.6
  (665 shorter events, 328.9 us)
Async XLA Ops:
  0.6 2.9 copy-start
  0.6 11.8 %copy-start.15 = (s32[1,2,640]{2,1,0:T(2,128)S(1)}, s32[1,2,640]{2,1,0:T(2,128)}, u32[]{:S(2)}) copy-start(s32[1,2,640]{2,1,0:T(2,128)} %param.30) | copy-start | bytes 15364
  1.4 11.1 %copy-start.25 = (s32[128]{0:T(128)}, s32[128]{0:T(128)S(1)}, u32[]{:S(2)}) copy-start(s32[128]{0:T(128)S(1)} %get-tuple-element.417) | copy-start | bytes 1540
  1.4 11.1 %copy-start.27 = (s32[128]{0:T(128)}, s32[128]{0:T(128)S(1)}, u32[]{:S(2)}) copy-start(s32[128]{0:T(128)S(1)} %get-tuple-element.418) | copy-start | bytes 1540
  3.6 8.9 %copy-start.36 = (pred[128]{0:T(512)(128)(4,1)}, pred[128]{0:T(512)(128)(4,1)S(1)}, u32[]{:S(2)}) copy-start(pred[128]{0:T(512)(128)(4,1)S(1)} %iota_compare_fusion.35) | copy-start | bytes 388
  5.0 22.1 %collective-permute-start.4 = (bf16[128,128]{1,0:T(8,128)(2,1)S(1)}, bf16[128,128]{1,0:T(8,128)(2,1)S(1)}, u32[]{:S(2)}, u32[]{:S(2)}) collective-permute-start(bf16[128,128]{1,0:T(8,128)(2,1)S(1)} %convolution_convert_fusion.5), channel_id=1, source_target_pairs={{0,1},{1,0},{2,3},{3,2},{4,5},{5,4},{6,7},{7,6},{8,9},{9,8},{10,11... | collective-permute-start | bytes 98312 | tf_op jit(solution)/shard_map/ppermute | solution.py:16
  7.0 20.1 %collective-permute-start.5 = (bf16[128,128]{1,0:T(8,128)(2,1)S(1)}, bf16[128,128]{1,0:T(8,128)(2,1)S(1)}, u32[]{:S(2)}, u32[]{:S(2)}) collective-permute-start(bf16[128,128]{1,0:T(8,128)(2,1)S(1)} %convolution_convert_fusion.4), channel_id=1, source_target_pairs={{0,1},{1,0},{2,3},{3,2},{4,5},{5,4},{6,7},{7,6},{8,9},{9,8},{10,11... | collective-permute-start | bytes 98312 | tf_op jit(solution)/shard_map/ppermute | solution.py:16
  7.8 4.7 copy-start.23
  7.8 11.3 %copy-start.21 = (s32[1,1,256]{2,1,0:T(1,128)}, s32[1,1,256]{2,1,0:T(1,128)S(1)}, u32[]{:S(2)}) copy-start(s32[1,1,256]{2,1,0:T(1,128)S(1)} %get-tuple-element.415) | copy-start | bytes 3076
  8.5 3.4 copy-start.40
  8.8 10.4 %copy-start.29 = (s32[640]{0:T(1024)S(1)}, s32[640]{0:T(1024)}, u32[]{:S(2)}) copy-start(s32[640]{0:T(1024)} %param.29) | copy-start | bytes 7684
  8.8 10.4 %copy-start.30 = (f32[100]{0:T(128)S(1)}, f32[100]{0:T(128)}, u32[]{:S(2)}) copy-start(f32[100]{0:T(128)} %param.46) | copy-start | bytes 1204
  8.8 15.5 %collective-permute-start.2 = (bf16[256,128]{1,0:T(8,128)(2,1)S(1)}, bf16[256,128]{1,0:T(8,128)(2,1)S(1)}, u32[]{:S(2)}, u32[]{:S(2)}) collective-permute-start(bf16[256,128]{1,0:T(8,128)(2,1)S(1)} %convolution_convert_fusion.3), channel_id=1, source_target_pairs={{0,2},{2,0},{1,3},{3,1},{4,6},{6,4},{5,7},{7,5},{8,10},{10,8},{9,1... | collective-permute-start | bytes 196616 | tf_op jit(solution)/shard_map/ppermute | solution.py:16
  12.4 6.4 copy-start.32
  12.5 2.8 copy-start.19
  12.5 6.7 copy-start.17
  12.5 7.1 copy-start.31
  12.5 8.8 %copy-start.16 = (s32[640]{0:T(1024)S(1)}, s32[640]{0:T(1024)}, u32[]{:S(2)}) copy-start(s32[640]{0:T(1024)} %param.28) | copy-start | bytes 7684
  12.5 9.5 %copy-start.11 = (s32[30720]{0:T(1024)S(1)}, s32[30720]{0:T(1024)}, u32[]{:S(2)}) copy-start(s32[30720]{0:T(1024)} %param.27) | copy-start | bytes 368644
  13.1 9.7 %collective-permute-start = (bf16[640,128]{1,0:T(8,128)(2,1)S(1)}, bf16[640,128]{1,0:T(8,128)(2,1)S(1)}, u32[]{:S(2)}, u32[]{:S(2)}) collective-permute-start(bf16[640,128]{1,0:T(8,128)(2,1)S(1)} %fusion.82), channel_id=1, source_target_pairs={{0,4},{4,8},{8,12},{12,0},{1,5},{5,9},{9,13},{13,1},{2,6},{6,10},{... | collective-permute-start | bytes 491528 | tf_op jit(solution)/shard_map/ppermute | solution.py:16
  15.3 3.5 copy-start.34
  15.3 11.7 %copy-start.2 = (bf16[128,128]{1,0:T(8,128)(2,1)S(1)}, bf16[128,128]{1,0:T(8,128)(2,1)}, u32[]{:S(2)}) copy-start(bf16[128,128]{1,0:T(8,128)(2,1)} %param.39) | copy-start | bytes 98308
  15.9 8.5 %collective-permute-start.1 = (bf16[640,128]{1,0:T(8,128)(2,1)S(1)}, bf16[640,128]{1,0:T(8,128)(2,1)S(1)}, u32[]{:S(2)}, u32[]{:S(2)}) collective-permute-start(bf16[640,128]{1,0:T(8,128)(2,1)S(1)} %fusion.79), channel_id=1, source_target_pairs={{0,12},{4,0},{8,4},{12,8},{1,13},{5,1},{9,5},{13,9},{2,14},{6,2},{... | collective-permute-start | bytes 491528 | tf_op jit(solution)/shard_map/ppermute | solution.py:16
  22.7 4.3 collective-permute-start.3
  61.9 2.4 copy-start.3
  61.9 2.5 copy-start.1
  68.3 7.5 copy-start.9
  132.9 2.5 copy-start.1
  139.4 7.5 copy-start.9
  204.0 2.5 copy-start.1
  210.4 7.5 copy-start.9
  275.0 2.5 copy-start.1
  281.4 7.5 copy-start.9
  346.0 2.5 copy-start.1
  352.5 7.5 copy-start.9
  417.1 2.5 copy-start.1
  423.5 7.5 copy-start.9
  488.2 2.5 copy-start.1
  494.6 7.5 copy-start.9
  559.2 2.5 copy-start.1
  565.7 7.5 copy-start.9
  630.2 2.5 copy-start.1
  636.6 7.5 copy-start.9
  701.3 2.4 copy-start.3
  701.3 2.5 copy-start.1
  707.7 7.5 copy-start.9
  743.7 7.6 copy-start.28
  743.7 7.6 copy-start.37
  743.8 7.9 %copy-start.26 = (s32[128]{0:T(128)S(1)}, s32[128]{0:T(128)}, u32[]{:S(2)}) copy-start(s32[128]{0:T(128)} %copy-done.25) | copy-start | bytes 1540
  743.8 7.9 %copy-start.39 = (pred[128]{0:T(512)(128)(4,1)S(1)}, pred[128]{0:T(512)(128)(4,1)}, u32[]{:S(2)}) copy-start(pred[128]{0:T(512)(128)(4,1)} %copy-done.38) | copy-start | bytes 388
  743.8 8.2 %copy-start.24 = (s32[1,1,256]{2,1,0:T(1,128)S(1)}, s32[1,1,256]{2,1,0:T(1,128)}, u32[]{:S(2)}) copy-start(s32[1,1,256]{2,1,0:T(1,128)} %copy-done.23) | copy-start | bytes 3076
  743.8 8.2 %copy-start.41 = (pred[256]{0:T(512)(128)(4,1)S(1)}, pred[256]{0:T(512)(128)(4,1)}, u32[]{:S(2)}) copy-start(pred[256]{0:T(512)(128)(4,1)} %copy-done.40) | copy-start | bytes 772
  743.8 10.2 %copy-start.22 = (s32[1,1,256]{2,1,0:T(1,128)S(1)}, s32[1,1,256]{2,1,0:T(1,128)}, u32[]{:S(2)}) copy-start(s32[1,1,256]{2,1,0:T(1,128)} %copy-done.21) | copy-start | bytes 3076
  743.8 10.2 %copy-start.43 = (pred[256]{0:T(512)(128)(4,1)S(1)}, pred[256]{0:T(512)(128)(4,1)}, u32[]{:S(2)}) copy-start(pred[256]{0:T(512)(128)(4,1)} %copy-done.42) | copy-start | bytes 772
  743.8 16.1 %copy-start.20 = (s32[640]{0:T(1024)S(1)}, s32[640]{0:T(1024)}, u32[]{:S(2)}) copy-start(s32[640]{0:T(1024)} %copy-done.19) | copy-start | bytes 7684
  743.8 16.1 %copy-start.35 = (pred[640]{0:T(1024)(128)(4,1)S(1)}, pred[640]{0:T(1024)(128)(4,1)}, u32[]{:S(2)}) copy-start(pred[640]{0:T(1024)(128)(4,1)} %copy-done.34) | copy-start | bytes 1924
  743.9 20.9 %copy-start.18 = (s32[640]{0:T(1024)S(1)}, s32[640]{0:T(1024)}, u32[]{:S(2)}) copy-start(s32[640]{0:T(1024)} %copy-done.17) | copy-start | bytes 7684
  743.9 20.9 %copy-start.33 = (pred[640]{0:T(1024)(128)(4,1)S(1)}, pred[640]{0:T(1024)(128)(4,1)}, u32[]{:S(2)}) copy-start(pred[640]{0:T(1024)(128)(4,1)} %copy-done.32) | copy-start | bytes 1924
  743.9 3.6 collective-permute-start.10
  745.2 6.5 collective-permute-start.11
  745.4 6.6 collective-permute-start.8
  745.8 8.2 %collective-permute-start.9 = (f32[3,256]{0,1:T(8,128)S(1)}, f32[3,256]{0,1:T(8,128)S(1)}, u32[]{:S(2)}, u32[]{:S(2)}) collective-permute-start(f32[3,256]{0,1:T(8,128)S(1)} %get-tuple-element.412), channel_id=1, source_target_pairs={{0,2},{2,0},{1,3},{3,1},{4,6},{6,4},{5,7},{7,5},{8,10},{10,8},{9,1... | collective-permute-start | bytes 9224 | tf_op jit(solution)/shard_map/ppermute | solution.py:16
  747.5 12.4 %collective-permute-start.7 = (f32[3,640]{0,1:T(8,128)S(1)}, f32[3,640]{0,1:T(8,128)S(1)}, u32[]{:S(2)}, u32[]{:S(2)}) collective-permute-start(f32[3,640]{0,1:T(8,128)S(1)} %get-tuple-element.409), channel_id=1, source_target_pairs={{0,4},{4,8},{8,12},{12,0},{1,5},{5,9},{9,13},{13,1},{2,6},{6,10},{... | collective-permute-start | bytes 23048 | tf_op jit(solution)/shard_map/ppermute | solution.py:16
  747.5 17.3 %collective-permute-start.6 = (f32[3,640]{0,1:T(8,128)S(1)}, f32[3,640]{0,1:T(8,128)S(1)}, u32[]{:S(2)}, u32[]{:S(2)}) collective-permute-start(f32[3,640]{0,1:T(8,128)S(1)} %get-tuple-element.410), channel_id=1, source_target_pairs={{0,12},{4,0},{8,4},{12,8},{1,13},{5,1},{9,5},{13,9},{2,14},{6,2},{... | collective-permute-start | bytes 23048 | tf_op jit(solution)/shard_map/ppermute | solution.py:16
  (82 other events, 141.0 us)
where the time goes:
time: 774 us; the launch traced here: 766 us
  other arithmetic  290 us (37%)
  local copies, waits for them, and re-layouts  278 us (36%)
  matrix products  166 us (21%)
  waiting for transfers between devices  15.1 us (2%)
  starting transfers between devices  14 us (2%)
    reduce_sum x10, other arithmetic, spread_terms(): summed = jnp.sum(summed.reshape(groups * UNIT_ROWS, 3, 3), axis=1)  129 us
    gather x10, local copies, waits for them, and re-layouts, block_terms(): neighbour_rows = table[index_rows].astype(jnp.float32)  91.6 us
    mul x10, local copies, waits for them, and re-layouts, spread_terms(): lower_onehot[:, :, None] * parts.T[:, None, :]  75.1 us
    reshape x10, local copies, waits for them, and re-layouts, spread_terms(): summed = jnp.sum(summed.reshape(groups * UNIT_ROWS, 3, 3), axis=1)  48.4 us
    reduce_sum x10, other arithmetic, block_terms(): jnp.sum(pair_grad * filter_out, axis=1) * envelope_slope  38.5 us
    dot_general x10, matrix products, spread_terms(): lax.dot_general(upper_onehot, placed, (((0,), (0,)), ((), ())), preferred...  35.5 us
    mul x10, other arithmetic, spread_terms(): lower_onehot[:, :, None] * parts.T[:, None, :]  31.1 us
    dynamic_update_slice x30, local copies, waits for them, and re-layouts, body(): lax.map(one_block, (features.reshape(block_total, block_rows, width), dis...  30.8 us
  transfers between devices with their start and end apart: 12, of which 5 were waited for; matrix products, arithmetic and copies ran while one was open for 2% of the time, Pallas kernels for 0%

commit v1 on v0

v1 whole, which is shorter than its diff:
```python
import math

import jax
import jax.numpy as jnp
from jax import lax
from jax.experimental import pallas as pl
from jax.experimental.pallas import tpu as pltpu
from jax.sharding import PartitionSpec as P

GAMMA = 10.0
CUTOFF = 5.0
LOG_TWO = math.log(2.0)
LOG2E = 1.0 / LOG_TWO
LANES = 128
UNROLL = 4
PIECES = 4
CHUNK = 256
RADIAL_ROWS = 64
GROUP_ROWS = 24

BF16 = jnp.bfloat16
F32 = jnp.float32


def dot(a, b):
    return jnp.dot(a, b, preferred_element_type=F32)


def dot_nt(a, b):
    return lax.dot_general(a, b, (((1,), (1,)), ((), ())), preferred_element_type=F32)


def split3(value):
    high = value.astype(BF16)
    rest = value - high.astype(F32)
    middle = rest.astype(BF16)
    low = (rest - middle.astype(F32)).astype(BF16)
    return high, middle, low


def softplus_of(value):
    return jnp.maximum(value, 0.0) + jnp.log(1.0 + jnp.exp(-jnp.abs(value)))


def sigmoid_of(value):
    return 1.0 / (1.0 + jnp.exp(-value))


def flip(weight):
    return weight.astype(F32).T.astype(BF16)


def pair_kernel(
    disp_ref,
    index_ref,
    count_ref,
    species_ref,
    scale_ref,
    shift_ref,
    feat_ref,
    table_ref,
    w1_ref,
    b1_ref,
    w2_ref,
    wo1_ref,
    wo2_ref,
    we1_ref,
    bf2_ref,
    bo1_ref,
    bo2_ref,
    be1_ref,
    w_e2_ref,
    energy_ref,
    own_ref,
    spread_ref,
    dist_ref,
    env_ref,
    row_ref,
    s1_ref,
    s2_ref,
    msg_ref,
    gm_ref,
    xj_ref,
    prod_ref,
    sig_ref,
    slope_ref,
    pf_ref,
    piece_ref,
    total_ref,
):
    slots, atoms = index_ref.shape
    width = feat_ref.shape[1]
    piece_rows = piece_ref.shape[1]
    tiles = atoms // LANES
    steps = slots // UNROLL
    span = UNROLL * LANES
    radial = w1_ref.shape[0]

    table_rows = table_ref.shape[1]
    for q in range(PIECES):
        have = max(0, min(piece_rows, table_rows - q * piece_rows))
        band = slice(q * width, (q + 1) * width)
        if have:
            piece_ref[band, 0:have] = table_ref[:, q * piece_rows : q * piece_rows + have]
        if have < piece_rows:
            piece_ref[band, have:piece_rows] = jnp.zeros((width, piece_rows - have), BF16)

    atom_row = lax.broadcasted_iota(jnp.int32, (1, atoms), 1)
    atom_col = lax.broadcasted_iota(jnp.int32, (atoms, 1), 0)
    count_row = count_ref[...].reshape(1, atoms)
    key_row = (count_row * atoms - atom_row).astype(F32)
    count_col = jnp.broadcast_to(count_row.astype(F32), (128, atoms)).T[:, 0:1]
    key_col = count_col * float(atoms) - atom_col.astype(F32)
    rank_col = jnp.sum(jnp.where(key_row > key_col, 1.0, 0.0), axis=1, keepdims=True)
    perm = jnp.where(rank_col == atom_row.astype(F32), 1.0, 0.0).astype(BF16)

    def sort_exact(value):
        high, middle, low = split3(value)
        return dot(high, perm) + dot(middle, perm) + dot(low, perm)

    def unsort_exact(value):
        high, middle, low = split3(value)
        return dot_nt(high, perm) + dot_nt(middle, perm) + dot_nt(low, perm)

    def put(ref, value):
        for s in range(steps):
            ref[s] = value[s * UNROLL : (s + 1) * UNROLL]

    def take(ref):
        return jnp.concatenate([ref[s] for s in range(steps)], axis=0)

    disp = sort_exact(disp_ref[...])
    index = index_ref[...]
    index_high = dot((index >> 7).astype(F32).astype(BF16), perm)
    index_low = dot((index & 127).astype(F32).astype(BF16), perm)
    put(row_ref, index_high * 128.0 + index_low)
    counts = dot(
        jnp.broadcast_to(count_row, (8, atoms)).astype(F32).astype(BF16), perm
    )[0:1]
    kinds = scale_ref.shape[0]
    kind_ids = lax.broadcasted_iota(jnp.int32, (kinds, 1), 0)
    kind_pick = jnp.where(kind_ids == species_ref[...].reshape(1, atoms), 1.0, 0.0).astype(BF16)
    pair_of = jnp.concatenate(
        [
            jnp.broadcast_to(scale_ref[...].reshape(1, kinds), (8, kinds)),
            jnp.broadcast_to(shift_ref[...].reshape(1, kinds), (8, kinds)),
        ],
        axis=0,
    )
    atom_vals = sort_exact(sum(dot(part, kind_pick) for part in split3(pair_of)))
    scale = atom_vals[0:1]
    shift = atom_vals[8:9]
    feat = dot(feat_ref[...].astype(F32).T.astype(BF16), perm)

    dx = disp[0:slots]
    dy = disp[slots : 2 * slots]
    dz = disp[2 * slots : 3 * slots]
    squared = dx * dx + dy * dy + dz * dz
    distance = jnp.sqrt(squared)
    put(dist_ref, distance)
    slot_ids = lax.broadcasted_iota(jnp.int32, (slots, 1), 0).astype(F32)
    live = jnp.where(slot_ids < counts, 1.0, 0.0)
    y = (math.pi / CUTOFF) * distance - 0.5 * math.pi
    y2 = y * y
    sin_y = y * (
        1.0
        + y2
        * (
            -1.0 / 6
            + y2 * (1.0 / 120 + y2 * (-1.0 / 5040 + y2 * (1.0 / 362880 - y2 * (1.0 / 39916800))))
        )
    )
    envelope = (0.5 - 0.5 * sin_y) * live
    put(env_ref, envelope)
    s1_ref[...] = jnp.zeros_like(s1_ref)
    s2_ref[...] = jnp.zeros_like(s2_ref)

    bias = b1_ref[...].reshape(1, width)
    bias_high = bias.astype(BF16).astype(F32)
    bias_middle = (bias - bias_high).astype(BF16).astype(F32)
    w1 = jnp.concatenate(
        [
            w1_ref[...].astype(F32),
            bias_high,
            bias_middle,
            bias - bias_high - bias_middle,
            jnp.zeros((RADIAL_ROWS - radial - 3, width), F32),
        ],
        axis=0,
    )
    w1t = w1.T.astype(BF16)
    radial_col = lax.broadcasted_iota(jnp.int32, (RADIAL_ROWS, 1), 0)
    w1_back = jnp.where(radial_col < radial, w1, 0.0).astype(BF16)
    mu = radial_col.astype(F32) * (CUTOFF / (radial - 1))
    sharp = jnp.where(radial_col < radial, -GAMMA * LOG2E, 0.0)
    w2 = w2_ref[...]
    w2t = flip(w2)

    def column(ref):
        size = ref.shape[0]
        return jnp.broadcast_to(ref[...].reshape(1, size), (128, size)).T[:, 0:1]

    b_f2 = column(bf2_ref) * LOG2E
    b_o1 = column(bo1_ref)
    b_o2 = column(bo2_ref)
    b_e1 = column(be1_ref)
    w_e2 = column(w_e2_ref)

    def lane_row(ref, step, tile):
        return jnp.concatenate(
            [
                ref[step, u : u + 1, tile * LANES : (tile + 1) * LANES]
                for u in range(UNROLL)
            ],
            axis=1,
        )

    sizes = []
    left = piece_rows
    while left > 0:
        sizes.append(min(CHUNK, left))
        left -= sizes[-1]

    def gather(row):
        piece = jnp.zeros_like(row)
        for q in range(1, PIECES):
            piece = piece + jnp.where(row >= float(q * piece_rows), 1.0, 0.0)
        local = row - piece * float(piece_rows)
        parts = []
        start = 0
        for size in sizes:
            inside = (local >= float(start)) & (local < float(start + size))
            spot = jnp.where(inside, local - float(start), -1.0)
            spot = jnp.broadcast_to(spot, (16, span)).astype(BF16)
            lanes = lax.broadcasted_iota(jnp.int32, (16, span), 0).astype(F32)
            for b in range(size // 16):
                ids = (lanes + float(16 * b)).astype(BF16)
                parts.append(
                    jnp.where(ids == spot, jnp.ones((), BF16), jnp.zeros((), BF16))
                )
            start += size
        onehot = jnp.concatenate(parts, axis=0)
        found = dot(piece_ref[...], onehot)
        out = found[0:width]
        for q in range(1, PIECES):
            out = jnp.where(piece == float(q), found[q * width : (q + 1) * width], out)
        return out

    trips = []
    for tile in range(tiles):
        most = jnp.max(counts[:, tile * LANES : (tile + 1) * LANES]).astype(jnp.int32)
        trips.append((most + (UNROLL - 1)) // UNROLL)

    for tile in range(tiles):
        lanes = slice(tile * LANES, (tile + 1) * LANES)
        msg_ref[:, lanes] = jnp.zeros((width, LANES), F32)

        def forward(step, carry, tile=tile, lanes=lanes):
            at = tile * steps + step
            offset = lane_row(dist_ref, step, tile) - mu
            basis = jnp.exp2(sharp * (offset * offset))
            slope_ref[at] = (offset * basis).astype(BF16)
            pre = dot(w1t, basis.astype(BF16))
            grown = jnp.exp2(pre * LOG2E)
            total = 1.0 + grown
            sig_ref[at] = (grown * pl.reciprocal(total, approx=True)).astype(BF16)
            hidden = (jnp.log2(total) - 1.0).astype(BF16)
            filt = dot(w2t, hidden) + b_f2
            xj = gather(lane_row(row_ref, step, tile))
            xj_ref[at] = xj.astype(BF16)
            prod = xj * filt
            prod_ref[at] = prod.astype(BF16)
            weighted = prod * lane_row(env_ref, step, tile)
            part = msg_ref[:, lanes]
            for u in range(UNROLL):
                part = part + weighted[:, u * LANES : (u + 1) * LANES]
            msg_ref[:, lanes] = part
            return carry

        lax.fori_loop(0, trips[tile], forward, 0)

    wo1 = wo1_ref[...]
    wo2 = wo2_ref[...]
    we1 = we1_ref[...]
    message = (msg_ref[...] * LOG_TWO).astype(BF16)
    out_pre = dot(flip(wo1), message) + b_o1
    out_mid = (softplus_of(out_pre) - LOG_TWO).astype(BF16)
    updated = (feat + dot(flip(wo2), out_mid) + b_o2).astype(BF16)
    energy_pre = dot(we1, updated) + b_e1
    soft = softplus_of(energy_pre) - LOG_TWO
    energy = scale * jnp.sum(soft * w_e2, axis=0, keepdims=True) + shift
    grad_head = (scale * w_e2 * sigmoid_of(energy_pre)).astype(BF16)
    grad_update = dot(flip(we1), grad_head).astype(BF16)
    grad_mid = (dot(wo2, grad_update) * sigmoid_of(out_pre)).astype(BF16)
    gm_ref[...] = dot(wo1, grad_mid)

    for tile in range(tiles):
        lanes = slice(tile * LANES, (tile + 1) * LANES)

        def backward(step, carry, tile=tile, lanes=lanes):
            at = tile * steps + step
            grad = gm_ref[:, lanes]
            grad_wide = jnp.concatenate([grad] * UNROLL, axis=1)
            grad_b = grad.astype(BF16)
            grad_b_wide = jnp.concatenate([grad_b] * UNROLL, axis=1)
            mixed = dot(w2, grad_b_wide * xj_ref[at])
            grad_pre = (mixed * sig_ref[at].astype(F32)).astype(BF16)
            grad_basis = dot(w1_back, grad_pre)
            s1 = jnp.sum(grad_basis * slope_ref[at].astype(F32), axis=0, keepdims=True)
            s2 = jnp.sum(grad_wide * prod_ref[at].astype(F32), axis=0, keepdims=True)
            for u in range(UNROLL):
                piece = slice(u * LANES, (u + 1) * LANES)
                s1_ref[step, u : u + 1, lanes] = s1[:, piece]
                s2_ref[step, u : u + 1, lanes] = s2[:, piece]
            return carry

        lax.fori_loop(0, trips[tile], backward, 0)

    cos_y = 1.0 + y2 * (
        -0.5
        + y2
        * (
            1.0 / 24
            + y2
            * (
                -1.0 / 720
                + y2 * (1.0 / 40320 + y2 * (-1.0 / 3628800 + y2 * (1.0 / 479001600)))
            )
        )
    )
    env_slope = (-0.5 * math.pi / CUTOFF * LOG_TWO) * cos_y
    grad_dist = envelope * (-2.0 * GAMMA) * take(s1_ref) + env_slope * take(s2_ref)
    ratio = jnp.where(live > 0.5, grad_dist / distance, 0.0)
    fx = dx * ratio
    fy = dy * ratio
    fz = dz * ratio
    put(pf_ref.at[0], fx)
    put(pf_ref.at[1], fy)
    put(pf_ref.at[2], fz)
    own = jnp.concatenate(
        [jnp.sum(fx, axis=0, keepdims=True), jnp.sum(fy, axis=0, keepdims=True),
         jnp.sum(fz, axis=0, keepdims=True), energy, jnp.zeros((4, atoms), F32)],
        axis=0,
    )
    plain = unsort_exact(own)
    own_ref[...] = plain
    energy_ref[...] = plain[3:4].reshape(atoms)

    total_ref[...] = jnp.zeros_like(total_ref)
    spread_ref[...] = jnp.zeros_like(spread_ref)

    def spread(step, carry):
        group = lax.broadcasted_iota(jnp.int32, (GROUP_ROWS, 1), 0).astype(F32)
        low_ids = lax.broadcasted_iota(jnp.int32, (128, 1), 0).astype(F32)
        total = total_ref[...]
        for u in range(UNROLL):
            row = row_ref[step, u : u + 1, :]
            high = jnp.floor(row * (1.0 / 128))
            low = row - high * 128.0
            here = group == high
            placed = jnp.concatenate(
                [jnp.where(here, -pf_ref[c, step, u : u + 1, :], 0.0) for c in range(3)], axis=0
            ).astype(BF16)
            lower = jnp.where(low_ids == low, 1.0, 0.0).astype(BF16)
            total = total + dot_nt(placed, lower)
        total_ref[...] = total
        return carry

    lax.fori_loop(0, steps, spread, 0)
    for c in range(3):
        spread_ref[:, c, :] = total_ref[c * GROUP_ROWS : (c + 1) * GROUP_ROWS]


def neighbours():
    found = []
    for axis in ("gx", "gy", "gz"):
        size = lax.axis_size(axis)
        place = lax.axis_index(axis)
        found.append({axis: lax.rem(place + 1, size)})
        found.append({axis: lax.rem(place + size - 1, size)})
    return found


def greet(found):
    barrier = pltpu.get_barrier_semaphore()
    for device in found:
        pl.semaphore_signal(
            barrier, inc=1, device_id=device, device_id_type=pl.DeviceIdType.MESH
        )
    pl.semaphore_wait(barrier, len(found))


def picker(list_row, used, atoms):
    lanes = lax.broadcasted_iota(jnp.int32, list_row.shape, 1)
    names = jnp.where(lanes < used, list_row, -1).astype(F32)
    ids = lax.broadcasted_iota(jnp.int32, (atoms, 1), 0).astype(F32)
    return jnp.where(ids == names, 1.0, 0.0).astype(BF16)


FACES = ((0, 1, 1, 0), (0, 0, 0, 1), (1, 1, 3, 2), (1, 0, 2, 3), (2, 1, 5, 4), (2, 0, 4, 5))


def send_kernel(
    feat_ref, w_ref, ex_ref, ey_ref, ez_ref, used_ref, table_ref, stage_ref, send_sem, recv_sem
):
    atoms = feat_ref.shape[0]
    lists = (ex_ref, ey_ref, ez_ref)
    found = neighbours()
    x = dot(feat_ref[...], w_ref[...])
    x_t = x.T.astype(BF16)
    used = used_ref[...]
    greet(found)
    copies = []
    start = 0
    for n, (dim, side, column, to) in enumerate(FACES):
        length = lists[dim].shape[1]
        pick = picker(lists[dim][side : side + 1, :], used[:, column : column + 1], atoms)
        stage_ref[:, start : start + length] = dot(x_t, pick).astype(BF16)
        copy = pltpu.make_async_remote_copy(
            src_ref=stage_ref.at[:, pl.ds(start, length)],
            dst_ref=table_ref.at[:, pl.ds(atoms + start, length)],
            send_sem=send_sem.at[n],
            recv_sem=recv_sem.at[n],
            device_id=found[to],
            device_id_type=pl.DeviceIdType.MESH,
        )
        copy.start()
        copies.append(copy)
        start += length
    table_ref[:, 0:atoms] = x_t
    for copy in copies:
        copy.wait()


def return_kernel(
    own_ref,
    spread_ref,
    ex_ref,
    ey_ref,
    ez_ref,
    used_ref,
    force_ref,
    land_ref,
    send_sem,
    recv_sem,
):
    atoms = force_ref.shape[1]
    lists = (ex_ref, ey_ref, ez_ref)
    found = neighbours()
    greet(found)
    copies = []
    group = atoms // 128
    start = 0
    for n, (dim, side, column, to) in enumerate(FACES):
        length = lists[dim].shape[1] // 128
        copy = pltpu.make_async_remote_copy(
            src_ref=spread_ref.at[pl.ds(group + start, length)],
            dst_ref=land_ref.at[pl.ds(start, length)],
            send_sem=send_sem.at[n],
            recv_sem=recv_sem.at[n],
            device_id=found[to ^ 1],
            device_id_type=pl.DeviceIdType.MESH,
        )
        copy.start()
        copies.append(copy)
        start += length
    total = own_ref[...] + jnp.concatenate([spread_ref[h] for h in range(group)], axis=1)
    used = used_ref[...]
    start = 0
    for n, (dim, side, column, to) in enumerate(FACES):
        length = lists[dim].shape[1] // 128
        pick = picker(lists[dim][side : side + 1, :], used[:, column : column + 1], atoms)
        copies[n].wait()
        values = jnp.concatenate([land_ref[start + h] for h in range(length)], axis=1)
        high, middle, low = split3(values)
        total = total + dot_nt(high, pick) + dot_nt(middle, pick) + dot_nt(low, pick)
        start += length
    force_ref[...] = total[0:3]


def body(
    features,
    displacement,
    neighbour,
    neighbour_count,
    species,
    exports_x,
    exports_y,
    exports_z,
    face_counts,
    w_in,
    w_f1,
    b_f1,
    w_f2,
    b_f2,
    w_o1,
    b_o1,
    w_o2,
    b_o2,
    w_e1,
    b_e1,
    w_e2,
    species_scale,
    species_shift,
):
    atom_rows, width = features.shape
    slot_count = neighbour.shape[0] // atom_rows
    used_counts = face_counts[0]
    vmem = pl.BlockSpec(memory_space=pltpu.VMEM)
    lists = (exports_x[0], exports_y[0], exports_z[0])
    ghost_rows = sum(2 * one.shape[1] for one in lists)
    table_rows = atom_rows + ghost_rows
    table_t = pl.pallas_call(
        send_kernel,
        out_shape=jax.ShapeDtypeStruct((width, table_rows), BF16),
        in_specs=[vmem] * 6,
        out_specs=vmem,
        scratch_shapes=[
            pltpu.VMEM((width, ghost_rows), BF16),
            pltpu.SemaphoreType.DMA((6,)),
            pltpu.SemaphoreType.DMA((6,)),
        ],
        compiler_params=pltpu.CompilerParams(
            collective_id=0, has_side_effects=True, vmem_limit_bytes=32 * 1024 * 1024
        ),
    )(features, w_in, *lists, face_counts)
    piece_rows = -(-table_rows // (PIECES * CHUNK)) * CHUNK
    disp_t = (
        displacement.reshape(3, atom_rows, slot_count).transpose(0, 2, 1).reshape(-1, atom_rows)
    )
    index_t = neighbour.reshape(atom_rows, slot_count).T
    steps = slot_count // UNROLL * (atom_rows // LANES)
    span = UNROLL * LANES
    energy, own_force, spread = pl.pallas_call(
        pair_kernel,
        out_shape=(
            jax.ShapeDtypeStruct((atom_rows,), F32),
            jax.ShapeDtypeStruct((8, atom_rows), F32),
            jax.ShapeDtypeStruct((GROUP_ROWS, 8, 128), F32),
        ),
        in_specs=[vmem] * 19,
        out_specs=(vmem, vmem, vmem),
        scratch_shapes=[
            pltpu.VMEM((slot_count // UNROLL, UNROLL, atom_rows), F32),
            pltpu.VMEM((slot_count // UNROLL, UNROLL, atom_rows), F32),
            pltpu.VMEM((slot_count // UNROLL, UNROLL, atom_rows), F32),
            pltpu.VMEM((slot_count // UNROLL, UNROLL, atom_rows), F32),
            pltpu.VMEM((slot_count // UNROLL, UNROLL, atom_rows), F32),
            pltpu.VMEM((width, atom_rows), F32),
            pltpu.VMEM((width, atom_rows), F32),
            pltpu.VMEM((steps, width, span), BF16),
            pltpu.VMEM((steps, width, span), BF16),
            pltpu.VMEM((steps, width, span), BF16),
            pltpu.VMEM((steps, RADIAL_ROWS, span), BF16),
            pltpu.VMEM((3, slot_count // UNROLL, UNROLL, atom_rows), F32),
            pltpu.VMEM((PIECES * width, piece_rows), BF16),
            pltpu.VMEM((3 * GROUP_ROWS, 128), F32),
        ],
        compiler_params=pltpu.CompilerParams(vmem_limit_bytes=56 * 1024 * 1024),
        cost_estimate=pl.CostEstimate(
            flops=30_000_000_000, bytes_accessed=4_000_000, transcendentals=16_000_000
        ),
    )(
        disp_t,
        index_t,
        neighbour_count,
        species,
        species_scale,
        species_shift,
        features,
        table_t,
        w_f1,
        b_f1,
        w_f2,
        w_o1,
        w_o2,
        w_e1.T,
        b_f2,
        b_o1,
        b_o2,
        b_e1,
        w_e2,
    )
    forces = pl.pallas_call(
        return_kernel,
        out_shape=jax.ShapeDtypeStruct((3, atom_rows), F32),
        in_specs=[vmem] * 6,
        out_specs=vmem,
        scratch_shapes=[
            pltpu.VMEM((ghost_rows // 128, 8, 128), F32),
            pltpu.SemaphoreType.DMA((6,)),
            pltpu.SemaphoreType.DMA((6,)),
        ],
        compiler_params=pltpu.CompilerParams(
            collective_id=1, has_side_effects=True, vmem_limit_bytes=32 * 1024 * 1024
        ),
    )(own_force, spread, *lists, face_counts)
    return (energy, forces)


def solution(mesh):
    both = ("geom", "gx", "gy", "gz")
    return jax.shard_map(
        body,
        mesh=mesh,
        in_specs=(
            P(both, None),
            P(None, both),
            P(both),
            P(both),
            P(both),
            P(both, None, None),
            P(both, None, None),
            P(both, None, None),
            P(both, None),
        )
        + (P(),) * 14,
        out_specs=(P(both), P(None, both)),
        check_vma=False,
    )
```

time: 774 us -> 95.8 us (0.12)
  other arithmetic: 290 us -> 0 us
  local copies, waits for them, and re-layouts: 278 us -> 7.3 us
  matrix products: 166 us -> 0 us
  Pallas kernels: 0 us -> 87.5 us
  waiting for transfers between devices: 15.1 us -> 0 us
  starting transfers between devices: 14 us -> 0 us
    reduce_sum x51 -> x0, other arithmetic: 205 us -> none  [the longest x10 129 us: spread_terms(): summed = jnp.sum(summed.reshape(groups * UNIT_ROWS, 3, 3), axis=1)]
    dot_general x95 -> x0, matrix products: 166 us -> none  [the longest x10 35.5 us: spread_terms(): lax.dot_general(upper_onehot, placed, (((0,), (0,)), ((), ())), preferred...]
    gather x10 -> x0, local copies, waits for them, and re-layouts: 91.6 us -> none  [block_terms(): neighbour_rows = table[index_rows].astype(jnp.float32)]
    pallas_call x0 -> x3, Pallas kernels: none -> 87.5 us  [the longest x1 64.9 us: body(): pl.pallas_call(pair_kernel, out_shape=(jax.ShapeDtypeStruct((atom_rows,),...]
    mul x10 -> x0, local copies, waits for them, and re-layouts: 75.1 us -> none  [spread_terms(): lower_onehot[:, :, None] * parts.T[:, None, :]]
    mul x40 -> x0, other arithmetic: 55.4 us -> none  [the longest x10 31.1 us: spread_terms(): lower_onehot[:, :, None] * parts.T[:, None, :]]
    reshape x16 -> x3, local copies, waits for them, and re-layouts: 51.8 us -> 2.44 us  [the longest x1 1.51 us: body(): displacement.reshape(3, atom_rows, slot_count).transpose(0, 2, 1)]
    dynamic_update_slice x30 -> x0, local copies, waits for them, and re-layouts: 30.8 us -> none  [body(): lax.map(one_block, (features.reshape(block_total, block_rows, width), dis...]
  transfers between devices with their start and end apart: 12 -> 0, of which waited for: 5 -> 0; matrix products, arithmetic and copies ran while one was open for 2% -> 0% of each run, Pallas kernels for 0% -> 0%
where the time goes in v1:
time: 95.8 us; the launch traced here: 95.5 us
  Pallas kernels  87.5 us (91%)
  local copies, waits for them, and re-layouts  7.3 us (8%)
    pallas_call x1, Pallas kernels, body(): pl.pallas_call(pair_kernel, out_shape=(jax.ShapeDtypeStruct((atom_rows,),...  64.9 us
    pallas_call x1, Pallas kernels, body(): pl.pallas_call(send_kernel, out_shape=jax.ShapeDtypeStruct((width, table_...  13.2 us
    pallas_call x1, Pallas kernels, body(): pl.pallas_call(return_kernel, out_shape=jax.ShapeDtypeStruct((3, atom_row...  9.42 us
    unnamed x21, local copies, waits for them, and re-layouts  3.8 us

profile of v1, /device:TPU:0, one launch (start us, length us, event | category | flops | bytes accessed | tf_op | source)
XLA Modules:
  0.0 95.5 jit_solution(17803901921370370103)
XLA Ops:
  0.6 1.5 %reshape.13 = f32[3,640,48]{2,1,0:T(8,128)S(1)} reshape(f32[3,30720]{1,0:T(4,128)} %param.24) | data formatting | bytes 737280 | tf_op jit(solution)/shard_map/reshape | solution.py:529
  2.1 0.0 copy-start.9
  2.2 1.1 %copy.26 = f32[3,48,640]{2,1,0:T(8,128)} copy(f32[3,48,640]{1,2,0:T(8,128)S(1)} %bitcast.13) | data formatting | bytes 737280 | tf_op jit(solution)/shard_map/transpose | solution.py:529
  3.2 0.0 copy-done.9
  3.2 0.2 reshape.15
  3.4 0.0 copy-start.1
  3.4 0.0 copy-start.3
  3.4 0.0 copy-start.7
  3.4 0.8 copy.27
  4.2 0.0 copy-start.4
  4.2 0.0 copy-start.6
  4.2 0.0 copy-start.8
  4.2 0.1 copy-done.1
  4.3 0.0 copy-done.3
  4.3 0.0 copy-done.7
  4.3 0.6 copy-done.4
  4.9 0.0 copy-done.6
  4.9 0.0 copy-done.8
  4.9 13.2 %shard_map.230.table_ref = bf16[128,2688]{1,0:T(8,128)(2,1)S(1)} custom-call(bf16[640,128]{1,0:T(8,128)(2,1)S(1)} %copy-done.1, bf16[128,128]{1,0:T(8,128)(2,1)S(1)} %copy-done.3, s32[2,640]{1,0:T(2,128)S(1)} %bitcast.7, s32[2,256]{1,0:T(2,128)S(1)} %bitcast.9, s32[2,128]{1,0:T(2,128)S(1)} %bitcast.11, s32[1,6]{1,0:T(1,128)S(1)} %copy-done.8), custom_call_target="tpu_custom_call" | custom-call | tf_op jit(solution)/shard_map/pallas_call | solution.py:513
  18.1 0.0 copy-start
  18.1 0.8 copy-done
  19.0 64.9 %shard_map.231 = (f32[640]{0:T(1024)}, f32[8,640]{1,0:T(8,128)}, f32[24,8,128]{2,1,0:T(8,128)}) custom-call(f32[144,640]{1,0:T(8,128)} %bitcast.14, s32[48,640]{1,0:T(8,128)} %bitcast.15, s32[640]{0:T(1024)} %count_ref.1, s32[640]{0:T(1024)} %species_ref.1, f32[100]{0:T(128)} %scale_ref.1, f32[100]{0:T(128)} %shift_ref.1, bf16[640,128]{1,0:T(8,128)(2,1)} %feat_ref.3, ...), custom_call_target="tpu_custom_call" | custom-call | flops 30000001024 | bytes 4000000 | tf_op jit(solution)/shard_map/pallas_call | solution.py:534
  83.8 0.0 copy-start.2
  83.8 0.9 copy-done.2
  84.7 0.0 copy-start.5
  84.7 0.7 copy-done.5
  85.4 9.4 %shard_map.232 = f32[3,640]{1,0:T(4,128)S(1)} custom-call(f32[8,640]{1,0:T(8,128)S(1)} %copy-done.5, f32[24,8,128]{2,1,0:T(8,128)S(1)} %copy-done.2, s32[2,640]{1,0:T(2,128)S(1)} %bitcast.8, s32[2,256]{1,0:T(2,128)S(1)} %bitcast.10, s32[2,128]{1,0:T(2,128)S(1)} %bitcast.12, s32[1,6]{1,0:T(1,128)S(1)} %copy-done.8), custom_call_target="tpu_custom_call" | custom-call | tf_op jit(solution)/shard_map/pallas_call | solution.py:584
  94.9 0.6 copy.29
Async XLA Ops:
  2.1 1.1 %copy-start.9 = (s32[30720]{0:T(1024)S(1)}, s32[30720]{0:T(1024)}, u32[]{:S(2)}) copy-start(s32[30720]{0:T(1024)} %param.25) | copy-start | bytes 368644
  3.4 0.9 copy-start.1
  3.4 0.9 copy-start.3
  3.4 0.9 copy-start.7
  4.2 0.7 copy-start.4
  4.2 0.7 copy-start.6
  4.2 0.7 copy-start.8
  18.1 0.8 copy-start
  83.8 0.9 copy-start.2
  84.7 0.7 copy-start.5
